TPU v7x, 32 devices: a whole 2x2x4 slice. The times are simulated.
32 devices in a mesh: az: 8 (over z, x), rg: 4 (over y, core).
Axes of the slice: x: 2, y: 2, z: 4, core: 2. Of those that a mesh axis runs over, the one named last changes fastest.
Arguments:
- echoes: bfloat16 [2, 2048, 32768], P(None, 'rg', 'az'), may hold values from -6 to 6
- coef_table: bfloat16 [8, 5, 128, 128], replicated, may hold values from -0.3125 to 0.3125
- kern_id: int32 [256], replicated, may hold values from 0 to 7
- band_lo: int32 [256], replicated, may hold values from -2 to 2, as said below
- band_width: int32 [256], replicated, may hold values from 1 to 5
- rate: float32 [2048], P('rg'), may hold values from 4 to 40
Outputs:
- image: bfloat16 [2, 2048, 32768], P(None, ('rg', 'az'))
Inputs may be any that keep to these rules, and one draw needn't show every extreme that they name: band_lo[b] + band_width[b] - 1 <= 2 for every frequency block b.
All inputs are finite; a program needn't handle non-finite values.
Results may differ from a plain program's by a relative error of at most 0.0095.
Values may be sent and summed in bfloat16 or wider, within the bound.
A program may use at most 128 MiB of HBM per device.

v0:
```python
import math

import jax
import jax.numpy as jnp
from jax import lax
from jax.sharding import PartitionSpec as P

A = 32768
P_SIZE = 512
Q = 64
TILE = 128
FB = 128
FBLK = 256
HT = 2
WMAX = 5


TWO_PI = 2.0 * math.pi


def padded_2(block, sides, width):
    for axis, dim in sides:
        count = lax.axis_size(axis)
        forward = [(i, i + 1) for i in range(count - 1)]
        backward = [(target, source) for source, target in forward]
        low = lax.ppermute(
            lax.slice_in_dim(block, block.shape[dim] - width, None, axis=dim), axis, forward
        )
        high = lax.ppermute(lax.slice_in_dim(block, 0, width, axis=dim), axis, backward)
        block = jnp.concatenate([low, block, high], axis=dim)
    return block


def rotation(first, second, length):
    product = lax.broadcasted_iota(jnp.int32, (first, second), 0) * lax.broadcasted_iota(
        jnp.int32, (first, second), 1
    )
    angle = (product % length).astype(jnp.float32) * (TWO_PI / length)
    return (jnp.cos(angle), jnp.sin(angle))


def tables():
    cosine_first, sine_first = rotation(P_SIZE, P_SIZE, P_SIZE)
    cosine_second, sine_second = rotation(Q, Q, Q)
    cosine_twist, sine_twist = rotation(Q, P_SIZE, A)
    scale_first = 1.0 / math.sqrt(P_SIZE)
    scale_second = 1.0 / math.sqrt(Q)
    return (
        (cosine_first * scale_first).astype(jnp.bfloat16),
        (sine_first * scale_first).astype(jnp.bfloat16),
        (cosine_second * scale_second).astype(jnp.bfloat16),
        (sine_second * scale_second).astype(jnp.bfloat16),
        cosine_twist,
        sine_twist,
    )


def contract(form, left, right):
    return jnp.einsum(form, left, right, preferred_element_type=jnp.float32)


def forward(planes, factors):
    cosine_first, sine_first, cosine_second, sine_second, cosine_twist, sine_twist = factors
    width = planes.shape[1]
    grid = planes.reshape(2, width, P_SIZE, Q)
    real_part = grid[0]
    imaginary = grid[1]
    first_real = contract("cpq,pf->cqf", real_part, cosine_first) + contract(
        "cpq,pf->cqf", imaginary, sine_first
    )
    first_imaginary = contract("cpq,pf->cqf", imaginary, cosine_first) - contract(
        "cpq,pf->cqf", real_part, sine_first
    )
    turned_real = (first_real * cosine_twist + first_imaginary * sine_twist).astype(jnp.bfloat16)
    turned_imaginary = (first_imaginary * cosine_twist - first_real * sine_twist).astype(
        jnp.bfloat16
    )
    second_real = contract("gq,cqf->cgf", cosine_second, turned_real) + contract(
        "gq,cqf->cgf", sine_second, turned_imaginary
    )
    second_imaginary = contract("gq,cqf->cgf", cosine_second, turned_imaginary) - contract(
        "gq,cqf->cgf", sine_second, turned_real
    )
    return jnp.stack([second_real, second_imaginary]).reshape(2, width, A).astype(jnp.bfloat16)


def inverse(planes, factors):
    cosine_first, sine_first, cosine_second, sine_second, cosine_twist, sine_twist = factors
    width = planes.shape[1]
    grid = planes.reshape(2, width, Q, P_SIZE)
    real_part = grid[0]
    imaginary = grid[1]
    first_real = contract("qg,cgf->cqf", cosine_second, real_part) - contract(
        "qg,cgf->cqf", sine_second, imaginary
    )
    first_imaginary = contract("qg,cgf->cqf", cosine_second, imaginary) + contract(
        "qg,cgf->cqf", sine_second, real_part
    )
    turned_real = (first_real * cosine_twist - first_imaginary * sine_twist).astype(jnp.bfloat16)
    turned_imaginary = (first_imaginary * cosine_twist + first_real * sine_twist).astype(
        jnp.bfloat16
    )
    second_real = contract("cqf,fp->cpq", turned_real, cosine_first) - contract(
        "cqf,fp->cpq", turned_imaginary, sine_first
    )
    second_imaginary = contract("cqf,fp->cpq", turned_imaginary, cosine_first) + contract(
        "cqf,fp->cpq", turned_real, sine_first
    )
    return jnp.stack([second_real, second_imaginary]).reshape(2, width, A).astype(jnp.bfloat16)


def body(echoes, coef_table, kern_id, band_lo, band_width, rate):
    factors = tables()
    members = lax.axis_size("az")
    here = lax.axis_index("az")
    range_rows = echoes.shape[1]
    lines = echoes.shape[2]
    columns = range_rows // members
    per_device = FBLK // members
    freq_dev = per_device * FB
    tiles = range_rows // TILE
    grouped = echoes.reshape(2, members, columns, lines)
    piece = lax.all_to_all(grouped, "az", split_axis=1, concat_axis=3, tiled=True)
    spectrum = forward(piece.reshape(2, piece.shape[2], A), factors)
    parted = spectrum.reshape(2, columns, members, freq_dev)
    turned = lax.all_to_all(parted, "az", split_axis=2, concat_axis=1, tiled=True)
    block_first = here * per_device
    block_stride = 1
    local = turned.reshape(2, range_rows, freq_dev)
    rim = HT * TILE
    padded = padded_2(local, (("rg", 1),), rim)

    def one_block(index, result):
        block = block_first + index * block_stride
        lower = band_lo[block]
        width = band_width[block]
        kernel = coef_table[kern_id[block]]
        columns_in = lax.dynamic_slice_in_dim(padded, index * FB, FB, 2)
        empty = jnp.zeros((2, tiles, TILE, FB), jnp.float32)
        total = empty
        for offset in range(WMAX):
            masked = jnp.where(offset < width, kernel[offset], jnp.zeros_like(kernel[offset]))
            start = (HT + lower + offset) * TILE
            slab = lax.dynamic_slice_in_dim(columns_in, start, range_rows, 1).reshape(
                2, tiles, TILE, FB
            )
            total = total + contract("ij,ptjf->ptif", masked, slab)
        moved = total.reshape(2, range_rows, FB)
        signed = (block * FB + lax.broadcasted_iota(jnp.int32, (FB,), 0) + A // 2) % A - A // 2
        doppler = signed.astype(jnp.float32) / A
        phase = rate[:, None] * (doppler * doppler)[None, :] * TWO_PI
        cosine = jnp.cos(phase)
        sine = jnp.sin(phase)
        focused_real = moved[0] * cosine + moved[1] * sine
        focused_imaginary = moved[1] * cosine - moved[0] * sine
        focused = jnp.stack([focused_real, focused_imaginary]).astype(jnp.bfloat16)
        return lax.dynamic_update_slice_in_dim(result, focused, index * FB, 2)

    filtered = lax.fori_loop(
        0, per_device, one_block, jnp.zeros((2, range_rows, freq_dev), jnp.bfloat16)
    )
    returned = filtered.reshape(2, members, columns, 1, freq_dev)
    piece = lax.all_to_all(returned, "az", split_axis=1, concat_axis=3, tiled=True)
    return inverse(piece.reshape(2, piece.shape[2], A), factors)


def solution(mesh):
    in_specs = (P(None, "rg", "az"), P(), P(), P(), P(), P("rg"))
    out_specs = P(None, ("rg", "az"), None)
    return jax.shard_map(body, mesh=mesh, in_specs=in_specs, out_specs=out_specs, check_vma=False)
```

profile of v0, /device:TPU:6, one launch (start us, length us, event | category | flops | bytes accessed | tf_op | source)
XLA Modules:
  0.0 1597.4 jit_solution(16955643325188588674)
XLA Ops:
  14.8 182.1 %all-to-all-done = bf16[2,8,64,4096]{3,2,0,1:T(8,128)(2,1)} async-done(((bf16[2,8,64,4096]{3,2,0,1:T(8,128)(2,1)}), bf16[2,8,64,4096]{3,2,0,1:T(8,128)(2,1)}, u32[]{:S(2)}, u32[]{:S(2)}) %all-to-all-start) | async-done | bytes 8388640 | tf_op jit(solution)/shard_map/all_to_all | solution.py:123
  206.3 12.5 squeeze.72
  218.8 8.5 copy.34
  227.3 10.8 fusion.69
  238.1 8.5 fusion.68
  250.8 12.5 squeeze.71
  263.4 8.5 copy.32
  271.9 10.6 fusion.67
  282.5 8.5 fusion.70
  291.0 13.4 fusion.48
  356.1 187.9 %all_to_all.45 = bf16[2,64,8,4096]{3,1,0,2:T(8,128)(2,1)} all-to-all(bf16[2,64,8,4096]{3,1,0,2:T(8,128)(2,1)} %pad_maximum_fusion.1), channel_id=1, replica_groups=mesh['az'=8,'rg'=4] {'az'}, dimensions={2} | all-to-all | bytes 16777216 | tf_op jit(solution)/shard_map/all_to_all | solution.py:126
  544.0 7.9 copy.39
  563.5 44.6 %collective-permute-done = bf16[2,256,4096]{2,1,0:T(8,128)(2,1)} collective-permute-done((bf16[2,256,4096]{2,1,0:T(8,128)(2,1)}, bf16[2,256,4096]{2,1,0:T(8,128)(2,1)}, u32[]{:S(2)}, u32[]{:S(2)}) %collective-permute-start) | collective-permute-done | bytes 4194336 | tf_op jit(solution)/shard_map/ppermute | solution.py:26
  609.8 13.6 pad_maximum_fusion
  627.9 681.1 %while.16 = (s32[]{:T(128)}, bf16[2,512,4096]{2,1,0:T(8,128)(2,1)}, s32[]{:T(128)}, s32[256]{0:T(256)S(1)}, bf16[2,1024,4096]{2,1,0:T(8,128)(2,1)}, /*index=5*/s...) while((s32[]{:T(128)}, bf16[2,512,4096]{2,1,0:T(8,128)(2,1)}, ...), condition=%wide.region_1.2_spmd, body=%wide.region_0.1_spmd.sunk | while | flops 169560240 | bytes 11180502 | solution.py:159
  1316.8 148.4 %all_to_all.46 = bf16[2,8,64,1,4096]{4,2,0,3,1:T(8,128)(2,1)S(1)} all-to-all(bf16[2,8,64,1,4096]{4,2,0,3,1:T(8,128)(2,1)} %copy.40), channel_id=1, replica_groups=mesh['az'=8,'rg'=4] {'az'}, dimensions={1} | all-to-all | bytes 16777216 | tf_op jit(solution)/shard_map/all_to_all | solution.py:163
  1506.4 9.6 fusion.44
  1523.7 8.3 fusion.63
  1532.0 8.1 fusion.53
  1540.1 8.5 copy.43
  1548.6 10.6 stack.39
  1559.2 11.2 fusion.54
  1570.4 8.3 copy.44
  1578.7 10.6 stack.40
  (475 shorter events, 550.2 us)
Async XLA Ops:
  7.9 188.9 %all-to-all-start = ((bf16[2,8,64,4096]{3,2,0,1:T(8,128)(2,1)}), bf16[2,8,64,4096]{3,2,0,1:T(8,128)(2,1)}, u32[]{:S(2)}, u32[]{:S(2)}) async-start(bf16[2,8,64,4096]{3,2,0,1:T(8,128)(2,1)} %copy.30), calls=%async_computation | async-start | bytes 16777216 | tf_op jit(solution)/shard_map/all_to_all | solution.py:123
  227.3 10.8 copy-start.8
  238.1 8.5 copy-start.5
  271.9 10.6 copy-start.9
  304.4 2.0 copy-start.2
  321.9 6.7 copy-start.3
  343.1 6.6 copy-start.7
  557.9 50.1 %collective-permute-start = (bf16[2,256,4096]{2,1,0:T(8,128)(2,1)}, bf16[2,256,4096]{2,1,0:T(8,128)(2,1)}, u32[]{:S(2)}, u32[]{:S(2)}) collective-permute-start(bf16[2,256,4096]{2,1,0:T(8,128)(2,1)} %get-tuple-element.312), channel_id=1, source_target_pairs={{0,1},{1,2},{2,3},{4,5},{5,6},{6,7},{8,9},{9,10},{10,11},{12,13},{... | collective-permute-start | bytes 12582920 | tf_op jit(solution)/shard_map/ppermute | solution.py:26
  559.8 50.0 %collective-permute-start.1 = (bf16[2,256,4096]{2,1,0:T(8,128)(2,1)}, bf16[2,256,4096]{2,1,0:T(8,128)(2,1)}, u32[]{:S(2)}, u32[]{:S(2)}) collective-permute-start(bf16[2,256,4096]{2,1,0:T(8,128)(2,1)} %get-tuple-element.313), channel_id=1, source_target_pairs={{1,0},{2,1},{3,2},{5,4},{6,5},{7,6},{9,8},{10,9},{11,10},{13,12},{... | collective-permute-start | bytes 12582920 | tf_op jit(solution)/shard_map/ppermute | solution.py:29
  623.4 4.5 copy-start.10
  623.4 4.5 copy-start.11
  623.5 4.5 copy-start.12
  623.5 4.5 copy-start.13
  1479.3 7.1 copy-start.1
  1486.4 4.6 copy-start.6
  1502.7 3.7 copy-start
  1516.0 7.7 copy-start.4
where the time goes:
time: 1630 us; the launch traced here: 1600 us
  local copies, waits for them, and re-layouts  350 us (21%)
  blocking collectives  336 us (21%)
  loops' own time  293 us (18%)
  matrix products  271 us (17%)
  waiting for transfers between devices  228 us (14%)
  other arithmetic  105 us (6%)
    another operation x1, loops' own time, body(): lax.fori_loop(0, per_device, one_block, jnp.zeros((2, range_rows, freq_de...  293 us
    dot_general x172, matrix products, contract(): return jnp.einsum(form, left, right, preferred_element_type=jnp.float32)  233 us
    all_to_all x1, blocking collectives, body(): lax.all_to_all(parted, 'az', split_axis=2, concat_axis=1, tiled=True)  188 us
    all_to_all x1, waiting for transfers between devices, body(): lax.all_to_all(grouped, 'az', split_axis=1, concat_axis=3, tiled=True)  182 us
    all_to_all x1, blocking collectives, body(): lax.all_to_all(returned, 'az', split_axis=1, concat_axis=3, tiled=True)  148 us
    dynamic_slice x32, local copies, waits for them, and re-layouts, one_block(): lax.dynamic_slice_in_dim(columns_in, start, range_rows, 1)  102 us
    ppermute x1, waiting for transfers between devices, padded_2(): lax.ppermute(lax.slice_in_dim(block, block.shape[dim] - width, None, axis...  44.6 us
    another operation x32, other arithmetic  40.1 us
  transfers between devices with their start and end apart: 3, of which 3 were waited for; matrix products, arithmetic and copies ran while one was open for 0% of the time, Pallas kernels for 0%

commit v1 on v0

v1 whole, which is shorter than its diff:
```python
import functools
import math

import jax
import jax.numpy as jnp
import numpy as np
import ml_dtypes
from jax import lax
from jax.experimental import pallas as pl
from jax.experimental.pallas import tpu as pltpu
from jax.sharding import PartitionSpec as P

A = 32768
HIGH = 256
LOW = 128
TILE = 128
FB = 128
HT = 2
WMAX = 5
TWO_PI = 2.0 * math.pi
VMEM = 48 * 1024 * 1024


def turn(first, second, length):
    product = np.arange(first)[:, None] * np.arange(second)[None, :]
    angle = (product % length) * (TWO_PI / length)
    return np.cos(angle), np.sin(angle)


def tables():
    c1, s1 = turn(HIGH, HIGH, HIGH)
    c1, s1 = c1 / math.sqrt(HIGH), s1 / math.sqrt(HIGH)
    c2, s2 = turn(LOW, LOW, LOW)
    c2, s2 = c2 / math.sqrt(LOW), s2 / math.sqrt(LOW)
    ct, st = turn(HIGH, LOW, A)
    bf = ml_dtypes.bfloat16
    first = np.block([[c1, s1], [-s1, c1]]).astype(bf)
    second = np.block([[c2, s2], [-s2, c2]]).astype(bf)
    second_back = np.block([[c2, -s2], [s2, c2]]).astype(bf)
    first_back = np.block([[c1, -s1], [s1, c1]]).astype(bf)
    ct, st = ct.astype(np.float32), st.astype(np.float32)
    return first, second, ct, st, second_back, first_back, ct.T.copy(), st.T.copy()


def circle():
    nodes = 0.5 * np.cos(np.pi * (np.arange(400) + 0.5) / 400)
    u = nodes * nodes
    sine = np.polynomial.Polynomial.fit(u, np.sin(TWO_PI * nodes) / nodes, 7, domain=[0, 0.25])
    cosine = np.polynomial.Polynomial.fit(u, np.cos(TWO_PI * nodes), 7, domain=[0, 0.25])
    return (
        [float(v) for v in sine.convert().coef],
        [float(v) for v in cosine.convert().coef],
    )


def horner(coefs, u):
    total = jnp.full_like(u, coefs[-1])
    for value in coefs[-2::-1]:
        total = total * u + value
    return total


def dot(left, right):
    return jnp.dot(left, right, preferred_element_type=jnp.float32)


def dot_t(left, right):
    return lax.dot_general(left, right, (((1,), (1,)), ((), ())), preferred_element_type=jnp.float32)


def forward_kernel(x_ref, first_ref, second_ref, ct_ref, st_ref, o_ref, held):
    rows = x_ref.shape[2]
    members, _, per, _, _ = o_ref.shape

    def pair(index, carry):
        both = []
        for j in range(2):
            r = index * 2 + j
            both.append(
                jnp.concatenate(
                    [x_ref[:, p, r].reshape(HIGH, LOW) for p in range(2)], axis=0
                )
            )
        y = dot(first_ref[...], jnp.concatenate(both, axis=1))
        for j in range(2):
            yr = y[:HIGH, j * LOW : (j + 1) * LOW]
            yi = y[HIGH:, j * LOW : (j + 1) * LOW]
            ct, st = ct_ref[...], st_ref[...]
            turned = jnp.concatenate(
                [
                    (yr * ct + yi * st).astype(jnp.bfloat16),
                    (yi * ct - yr * st).astype(jnp.bfloat16),
                ],
                axis=1,
            )
            held[index * 2 + j] = dot_t(second_ref[...], turned)
        return carry

    lax.fori_loop(0, rows // 2, pair, 0)
    for p in range(2):
        for d in range(members):
            lo = p * LOW + d * per
            piece = jnp.swapaxes(held[:, lo : lo + per, :], 0, 1)
            o_ref[d, p] = piece.astype(jnp.bfloat16)


def inverse_kernel(x_ref, second_ref, first_ref, ct_ref, st_ref, o_ref, held):
    members, _, per, rows, _ = x_ref.shape
    group = max(1, 16 // per)
    for p in range(2):
        for s in range(0, members, group):
            pieces = [
                jnp.swapaxes(x_ref[s + g, p].astype(jnp.float32), 0, 1) for g in range(group)
            ]
            piece = pieces[0] if group == 1 else jnp.concatenate(pieces, axis=1)
            lo = p * LOW + s * per
            held[:, lo : lo + group * per, :] = piece.astype(jnp.bfloat16)

    def pair(index, carry):
        both = []
        for j in range(2):
            u = dot(second_ref[...], held[index * 2 + j])
            ur, ui = u[:LOW], u[LOW:]
            ct, st = ct_ref[...], st_ref[...]
            both.append(
                jnp.concatenate(
                    [
                        (ur * ct - ui * st).astype(jnp.bfloat16),
                        (ui * ct + ur * st).astype(jnp.bfloat16),
                    ],
                    axis=1,
                )
            )
        out = dot_t(first_ref[...], jnp.concatenate(both, axis=0)).astype(jnp.bfloat16)
        for p in range(2):
            for j in range(2):
                o_ref[p, index * 2 + j] = out[p * HIGH : (p + 1) * HIGH, j * LOW : (j + 1) * LOW]
        return carry

    lax.fori_loop(0, rows // 2, pair, 0)


def migrate_kernel(
    place, kern_id, band_lo, band_width, low_ref, mid_ref, high_ref, coef_ref, rate_ref, o_ref, held
):
    sine_coefs, cosine_coefs = circle()
    step = pl.program_id(0)
    columns = mid_ref.shape[3]
    range_rows = mid_ref.shape[0] * columns
    rim = HT * TILE
    full = range_rows + 2 * rim
    halves = HIGH // FB

    @pl.when(step == 0)
    def _():
        held[full:, :] = jnp.zeros((held.shape[0] - full, held.shape[1]), held.dtype)

    row = 0
    for ref in (low_ref, mid_ref, high_ref):
        for s in range(ref.shape[0]):
            for p in range(2):
                for h in range(halves):
                    lane = (h * 2 + p) * FB
                    held[row : row + columns, lane : lane + FB] = ref[
                        s, p, 0, :, h * FB : (h + 1) * FB
                    ]
            row += columns

    for h in range(halves):
        block = place[0] + step * halves + h
        lower = band_lo[block]
        width = band_width[block]
        kernel = kern_id[block]
        weights = jnp.concatenate(
            [
                jnp.where(
                    k < width, coef_ref[kernel, k].astype(jnp.float32), 0.0
                ).astype(jnp.bfloat16)
                for k in range(WMAX)
            ],
            axis=1,
        )
        lanes = lax.broadcasted_iota(jnp.int32, (1, FB), 1)
        signed = (block * FB + lanes + A // 2) % A - A // 2
        doppler = signed.astype(jnp.float32) * (1.0 / A)
        squared = doppler * doppler
        for t in range(range_rows // TILE):
            start = pl.multiple_of((t + HT + lower) * TILE, TILE)
            moved = dot(
                weights, held[pl.ds(start, WMAX * TILE), h * 2 * FB : (h + 1) * 2 * FB]
            )
            turns = rate_ref[t * TILE : (t + 1) * TILE, :] * squared
            x = turns - jnp.round(turns)
            u = x * x
            sine = horner(sine_coefs, u) * x
            cosine = horner(cosine_coefs, u)
            mr, mi = moved[:, :FB], moved[:, FB:]
            done = (
                (mr * cosine + mi * sine).astype(jnp.bfloat16),
                (mi * cosine - mr * sine).astype(jnp.bfloat16),
            )
            for p in range(2):
                for part in range(TILE // columns):
                    o_ref[t * (TILE // columns) + part, p, 0, :, h * FB : (h + 1) * FB] = done[p][
                        part * columns : (part + 1) * columns
                    ]


def whole_spec(shape):
    return pl.BlockSpec(shape, lambda *_: (0,) * len(shape))


def params():
    return pltpu.CompilerParams(vmem_limit_bytes=VMEM)


def forward(x, first, second, ct, st):
    members, _, columns, fold, _ = x.shape
    per = LOW // members
    rows = min(16, columns)
    return pl.pallas_call(
        forward_kernel,
        grid=(columns // rows,),
        in_specs=[
            pl.BlockSpec((members, 2, rows, fold, LOW), lambda i: (0, 0, i, 0, 0)),
            whole_spec(first.shape),
            whole_spec(second.shape),
            whole_spec(ct.shape),
            whole_spec(st.shape),
        ],
        out_specs=pl.BlockSpec((members, 2, per, rows, HIGH), lambda i: (0, 0, 0, i, 0)),
        out_shape=jax.ShapeDtypeStruct((members, 2, per, columns, HIGH), jnp.bfloat16),
        scratch_shapes=[pltpu.VMEM((rows, 2 * LOW, HIGH), jnp.float32)],
        compiler_params=params(),
    )(x, first, second, ct, st)


def inverse(x, second, first, ct, st):
    members, _, per, columns, _ = x.shape
    rows = min(16, columns)
    return pl.pallas_call(
        inverse_kernel,
        grid=(columns // rows,),
        in_specs=[
            pl.BlockSpec((members, 2, per, rows, HIGH), lambda i: (0, 0, 0, i, 0)),
            whole_spec(second.shape),
            whole_spec(first.shape),
            whole_spec(ct.shape),
            whole_spec(st.shape),
        ],
        out_specs=pl.BlockSpec((2, rows, HIGH, LOW), lambda i: (0, i, 0, 0)),
        out_shape=jax.ShapeDtypeStruct((2, columns, HIGH, LOW), jnp.bfloat16),
        scratch_shapes=[pltpu.VMEM((rows, 2 * LOW, HIGH), jnp.bfloat16)],
        compiler_params=params(),
    )(x, second, first, ct, st)


def migrate(place, kern_id, band_lo, band_width, low, mid, high, coef, rate):
    members, _, per, columns, _ = mid.shape
    range_rows = members * columns
    depth = range_rows + (2 * HT + WMAX - 1) * TILE

    def chunk(count):
        return pl.BlockSpec((count, 2, 1, columns, HIGH), lambda i, *_: (0, 0, i, 0, 0))

    return pl.pallas_call(
        migrate_kernel,
        grid_spec=pltpu.PrefetchScalarGridSpec(
            num_scalar_prefetch=4,
            grid=(per,),
            in_specs=[
                chunk(low.shape[0]),
                chunk(members),
                chunk(high.shape[0]),
                whole_spec(coef.shape),
                whole_spec((range_rows, 1)),
            ],
            out_specs=chunk(members),
            scratch_shapes=[pltpu.VMEM((depth, 2 * HIGH), jnp.bfloat16)],
        ),
        out_shape=jax.ShapeDtypeStruct(mid.shape, jnp.bfloat16),
        compiler_params=params(),
    )(place, kern_id, band_lo, band_width, low, mid, high, coef, rate.reshape(-1, 1))


def exchange(block):
    return lax.all_to_all(block, "az", split_axis=0, concat_axis=0, tiled=True)


def body(echoes, coef_table, kern_id, band_lo, band_width, rate):
    first, second, ct, st, second_back, first_back, ct_back, st_back = map(jnp.asarray, tables())
    members = lax.axis_size("az")
    here = lax.axis_index("az")
    range_rows, lines = echoes.shape[1:]
    columns = range_rows // members
    per = LOW // members
    grouped = echoes.reshape(2, members, columns, lines // LOW, LOW).transpose(1, 0, 2, 3, 4)
    spectrum = exchange(forward(exchange(grouped), first, second, ct, st))
    chunks = HT * TILE // columns
    count = lax.axis_size("rg")
    up = [(i, i + 1) for i in range(count - 1)]
    down = [(i + 1, i) for i in range(count - 1)]
    low = lax.ppermute(spectrum[members - chunks :], "rg", up)
    high = lax.ppermute(spectrum[:chunks], "rg", down)
    place = (here * per * (HIGH // FB)).astype(jnp.int32).reshape(1)
    focused = migrate(
        place, kern_id, band_lo, band_width, low, spectrum, high, coef_table, rate
    )
    image = inverse(exchange(focused), second_back, first_back, ct_back, st_back)
    return image.reshape(2, columns, A)


def solution(mesh):
    in_specs = (P(None, "rg", "az"), P(), P(), P(), P(), P("rg"))
    out_specs = P(None, ("rg", "az"), None)
    return jax.shard_map(body, mesh=mesh, in_specs=in_specs, out_specs=out_specs, check_vma=False)
```

time: 1630 us -> 692 us (0.42); the launches traced: 1600 us -> 690 us
  local copies, waits for them, and re-layouts: 350 us -> 37.4 us
  loops' own time: 293 us -> 0 us
  matrix products: 271 us -> 0 us
  blocking collectives: 336 us -> 527 us
  waiting for transfers between devices: 228 us -> 45.6 us
  other arithmetic: 105 us -> 0 us
  Pallas kernels: 0 us -> 73.7 us
    another operation x1 -> x0, loops' own time: 293 us -> none  [body(): lax.fori_loop(0, per_device, one_block, jnp.zeros((2, range_rows, freq_de...]
    dot_general x172 -> x0, matrix products: 233 us -> none  [contract(): return jnp.einsum(form, left, right, preferred_element_type=jnp.float32)]
    all_to_all x2 -> x3, blocking collectives: 336 us -> 527 us  [exchange(): return lax.all_to_all(block, 'az', split_axis=0, concat_axis=0, tiled=True)]
    all_to_all x1 -> x0, waiting for transfers between devices: 182 us -> none  [body(): lax.all_to_all(grouped, 'az', split_axis=1, concat_axis=3, tiled=True)]
    dynamic_slice x128 -> x0, local copies, waits for them, and re-layouts: 167 us -> none  [the longest x32 102 us: one_block(): lax.dynamic_slice_in_dim(columns_in, start, range_rows, 1)]
    pallas_call x0 -> x3, Pallas kernels: none -> 73.7 us  [the longest x1 26.1 us: forward(): pl.pallas_call(forward_kernel, grid=(columns // rows,), in_specs=[pl.Bloc...]
    squeeze x6 -> x0, local copies, waits for them, and re-layouts: 56.9 us -> none  [the longest x2 21.1 us: forward(): imaginary = grid[1]]
    another operation x34 -> x0, other arithmetic: 54.1 us -> none
  transfers between devices with their start and end apart: 3 -> 2, of which waited for: 3 -> 2; matrix products, arithmetic and copies ran while one was open for 0% -> 0% of each run, Pallas kernels for 0% -> 0%
where the time goes in v1:
time: 692 us; the launch traced here: 690 us
  blocking collectives  527 us (76%)
  Pallas kernels  73.7 us (11%)
  waiting for transfers between devices  45.6 us (7%)
  local copies, waits for them, and re-layouts  37.4 us (5%)
    all_to_all x3, blocking collectives, exchange(): return lax.all_to_all(block, 'az', split_axis=0, concat_axis=0, tiled=True)  527 us
    ppermute x1, waiting for transfers between devices, body(): high = lax.ppermute(spectrum[:chunks], 'rg', down)  41.8 us
    pallas_call x1, Pallas kernels, forward(): pl.pallas_call(forward_kernel, grid=(columns // rows,), in_specs=[pl.Bloc...  26.1 us
    pallas_call x1, Pallas kernels, inverse(): pl.pallas_call(inverse_kernel, grid=(columns // rows,), in_specs=[pl.Bloc...  24.4 us
    pallas_call x1, Pallas kernels, migrate(): pl.pallas_call(migrate_kernel, grid_spec=pltpu.PrefetchScalarGridSpec(num...  23.3 us
  transfers between devices with their start and end apart: 2, of which 2 were waited for; matrix products, arithmetic and copies ran while one was open for 0% of the time, Pallas kernels for 0%

profile of v1, /device:TPU:6, one launch (start us, length us, event | category | flops | bytes accessed | tf_op | source)
XLA Modules:
  0.0 690.3 jit_solution(15026211741218881619)
XLA Ops:
  0.0 9.6 %copy.17 = bf16[128,8,32,128]{3,2,1,0:T(8,128)(2,1)} copy(bf16[128,8,32,128]{3,1,2,0:T(8,128)(2,1)} %bitcast.13) | data formatting | bytes 16777216
  9.6 8.5 %copy.19 = bf16[2,8,64,32,128]{4,3,2,0,1:T(8,128)(2,1)} copy(bf16[2,8,64,32,128]{4,3,2,1,0:T(8,128)(2,1)} %bitcast.12) | data formatting | bytes 16777216 | tf_op jit(solution)/shard_map/reshape | solution.py:297
  18.1 189.2 %all_to_all.15.x_ref = bf16[8,2,64,32,128]{4,3,2,1,0:T(8,128)(2,1)} all-to-all(bf16[8,2,64,32,128]{4,3,2,1,0:T(8,128)(2,1)} %bitcast.11), channel_id=1, replica_groups=mesh['az'=8,'rg'=4] {'az'}, dimensions={0} | all-to-all | bytes 16777216 | tf_op jit(solution)/shard_map/all_to_all | solution.py:287
  207.3 0.0 copy-done.2
  207.3 26.1 %shard_map.136 = bf16[8,2,16,64,256]{4,3,2,1,0:T(8,128)(2,1)} custom-call(bf16[8,2,64,32,128]{4,3,2,1,0:T(8,128)(2,1)} %all_to_all.15.x_ref, bf16[512,512]{1,0:T(8,128)(2,1)S(1)} %copy-done.2, bf16[256,256]{1,0:T(8,128)(2,1)S(1)} %copy-done.8, f32[256,128]{1,0:T(8,128)S(1)} %copy-done.7, f32[256,128]{1,0:T(8,128)S(1)} %copy-done.6), custom_call_target="tpu_custom_call" | custom-call | tf_op jit(solution)/shard_map/pallas_call | solution.py:221
  233.4 186.7 %all_to_all.16.mid_ref = bf16[8,2,16,64,256]{4,3,2,1,0:T(8,128)(2,1)S(1)} all-to-all(bf16[8,2,16,64,256]{4,3,2,1,0:T(8,128)(2,1)} %shard_map.136), channel_id=1, replica_groups=mesh['az'=8,'rg'=4] {'az'}, dimensions={0} | all-to-all | bytes 16777216 | tf_op jit(solution)/shard_map/all_to_all | solution.py:287
  420.1 0.0 copy-start.10
  420.1 0.0 copy-start.11
  420.1 3.8 fusion
  423.9 2.1 copy-done.12
  426.0 1.9 collective-permute-start.1
  427.9 4.3 collective-permute-start
  432.3 0.0 copy-done.13
  432.3 0.1 copy.16.rate_ref
  432.4 41.8 %collective-permute-done.1.high_ref = bf16[4,2,16,64,256]{4,3,2,1,0:T(8,128)(2,1)} collective-permute-done((bf16[4,2,16,64,256]{4,3,2,1,0:T(8,128)(2,1)}, bf16[4,2,16,64,256]{4,3,2,1,0:T(8,128)(2,1)}, u32[]{:S(2)}, u32[]{:S(2)}) %collective-permute-start.1) | collective-permute-done | bytes 4194336 | tf_op jit(solution)/shard_map/ppermute | solution.py:304
  474.2 3.8 collective-permute-done.low_ref
  478.1 0.0 copy-done
  478.1 0.0 copy-done.10
  478.1 23.3 %shard_map.137 = bf16[8,2,16,64,256]{4,3,2,1,0:T(8,128)(2,1)} custom-call(s32[1]{0:T(128)} %bitcast.place, s32[256]{0:T(256)S(1)} %copy-done.9, s32[256]{0:T(256)S(1)} %copy-done.10, s32[256]{0:T(256)S(1)} %copy-done.11, bf16[4,2,16,64,256]{4,3,2,1,0:T(8,128)(2,1)} %collective-permute-done.low_ref, bf16[8,2,16,64,256]{4,3,2,1,0:T(8,128)(2,1)} %copy-done.12, ...), custom_call_target="tpu_custom_call" | custom-call | tf_op jit(solution)/shard_map/pallas_call | solution.py:266
  501.4 0.0 copy-start.5
  501.4 151.2 %all_to_all.17.x_ref = bf16[8,2,16,64,256]{4,3,2,1,0:T(8,128)(2,1)} all-to-all(bf16[8,2,16,64,256]{4,3,2,1,0:T(8,128)(2,1)} %shard_map.137), channel_id=1, replica_groups=mesh['az'=8,'rg'=4] {'az'}, dimensions={0} | all-to-all | bytes 16777216 | tf_op jit(solution)/shard_map/all_to_all | solution.py:287
  652.6 0.0 copy-done.1
  652.6 24.4 %shard_map.138 = bf16[2,64,256,128]{3,2,1,0:T(8,128)(2,1)} custom-call(bf16[8,2,16,64,256]{4,3,2,1,0:T(8,128)(2,1)} %all_to_all.17.x_ref, bf16[256,256]{1,0:T(8,128)(2,1)S(1)} %copy-done.5, bf16[512,512]{1,0:T(8,128)(2,1)S(1)} %copy-done.1, f32[128,256]{1,0:T(8,128)S(1)} %copy-done.4, f32[128,256]{1,0:T(8,128)S(1)} %copy-done.3), custom_call_target="tpu_custom_call" | custom-call | tf_op jit(solution)/shard_map/pallas_call | solution.py:241
  677.1 13.3 %reshape.15 = bf16[2,64,32768]{2,1,0:T(8,128)(2,1)} reshape(bf16[2,64,256,128]{3,2,1,0:T(8,128)(2,1)} %shard_map.138) | data formatting | bytes 16777216 | tf_op jit(solution)/shard_map/reshape | solution.py:310
  (19 shorter events, 0.0 us)
Async XLA Ops:
  18.1 189.3 %copy-start.2 = (bf16[512,512]{1,0:T(8,128)(2,1)S(1)}, bf16[512,512]{1,0:T(8,128)(2,1)}, u32[]{:S(2)}) copy-start(bf16[512,512]{1,0:T(8,128)(2,1)} %constant.26.clone.first_ref) | copy-start | bytes 1572868
  18.1 189.3 %copy-start.6 = (f32[256,128]{1,0:T(8,128)S(1)}, f32[256,128]{1,0:T(8,128)}, u32[]{:S(2)}) copy-start(f32[256,128]{1,0:T(8,128)} %constant.29.clone.st_ref) | copy-start | bytes 393220
  18.1 189.3 %copy-start.7 = (f32[256,128]{1,0:T(8,128)S(1)}, f32[256,128]{1,0:T(8,128)}, u32[]{:S(2)}) copy-start(f32[256,128]{1,0:T(8,128)} %constant.28.clone.ct_ref) | copy-start | bytes 393220
  18.1 189.3 %copy-start.8 = (bf16[256,256]{1,0:T(8,128)(2,1)S(1)}, bf16[256,256]{1,0:T(8,128)(2,1)}, u32[]{:S(2)}) copy-start(bf16[256,256]{1,0:T(8,128)(2,1)} %constant.27.clone.second_ref) | copy-start | bytes 393220
  420.1 5.9 copy-start.12
  420.1 12.2 %copy-start.13 = (f32[512]{0:T(512)S(1)}, f32[512]{0:T(512)}, u32[]{:S(2)}) copy-start(f32[512]{0:T(512)} %param.19) | copy-start | bytes 6148
  420.1 58.0 %copy-start = (bf16[8,5,128,128]{3,2,1,0:T(8,128)(2,1)S(1)}, bf16[8,5,128,128]{3,2,1,0:T(8,128)(2,1)}, u32[]{:S(2)}) copy-start(bf16[8,5,128,128]{3,2,1,0:T(8,128)(2,1)} %coef_ref.1) | copy-start | bytes 3932164
  420.1 58.0 %copy-start.9 = (s32[256]{0:T(256)S(1)}, s32[256]{0:T(256)}, u32[]{:S(2)}) copy-start(s32[256]{0:T(256)} %kern_id.1) | copy-start | bytes 3076
  420.1 58.0 %copy-start.10 = (s32[256]{0:T(256)S(1)}, s32[256]{0:T(256)}, u32[]{:S(2)}) copy-start(s32[256]{0:T(256)} %band_lo.1) | copy-start | bytes 3076
  420.1 58.0 %copy-start.11 = (s32[256]{0:T(256)S(1)}, s32[256]{0:T(256)}, u32[]{:S(2)}) copy-start(s32[256]{0:T(256)} %band_width.1) | copy-start | bytes 3076
  426.0 48.2 %collective-permute-start.1 = (bf16[4,2,16,64,256]{4,3,2,1,0:T(8,128)(2,1)}, bf16[4,2,16,64,256]{4,3,2,1,0:T(8,128)(2,1)}, u32[]{:S(2)}, u32[]{:S(2)}) collective-permute-start(bf16[4,2,16,64,256]{4,3,2,1,0:T(8,128)(2,1)} %get-tuple-element.5), channel_id=1, source_target_pairs={{1,0},{2,1},{3,2},{5,4},{6,5},{7,6},{9,8},{10,9},{11,10},{13,12},{... | collective-permute-start | bytes 12582920 | tf_op jit(solution)/shard_map/ppermute | solution.py:304
  427.9 50.1 %collective-permute-start = (bf16[4,2,16,64,256]{4,3,2,1,0:T(8,128)(2,1)}, bf16[4,2,16,64,256]{4,3,2,1,0:T(8,128)(2,1)}, u32[]{:S(2)}, u32[]{:S(2)}) collective-permute-start(bf16[4,2,16,64,256]{4,3,2,1,0:T(8,128)(2,1)} %get-tuple-element.6), channel_id=1, source_target_pairs={{0,1},{1,2},{2,3},{4,5},{5,6},{6,7},{8,9},{9,10},{10,11},{12,13},{... | collective-permute-start | bytes 12582920 | tf_op jit(solution)/shard_map/ppermute | solution.py:303
  501.4 151.3 %copy-start.1 = (bf16[512,512]{1,0:T(8,128)(2,1)S(1)}, bf16[512,512]{1,0:T(8,128)(2,1)}, u32[]{:S(2)}) copy-start(bf16[512,512]{1,0:T(8,128)(2,1)} %constant.31.clone.first_ref) | copy-start | bytes 1572868
  501.4 151.3 %copy-start.3 = (f32[128,256]{1,0:T(8,128)S(1)}, f32[128,256]{1,0:T(8,128)}, u32[]{:S(2)}) copy-start(f32[128,256]{1,0:T(8,128)} %constant.33.clone.st_ref) | copy-start | bytes 393220
  501.4 151.3 %copy-start.4 = (f32[128,256]{1,0:T(8,128)S(1)}, f32[128,256]{1,0:T(8,128)}, u32[]{:S(2)}) copy-start(f32[128,256]{1,0:T(8,128)} %constant.32.clone.ct_ref) | copy-start | bytes 393220
  501.4 151.3 %copy-start.5 = (bf16[256,256]{1,0:T(8,128)(2,1)S(1)}, bf16[256,256]{1,0:T(8,128)(2,1)}, u32[]{:S(2)}) copy-start(bf16[256,256]{1,0:T(8,128)(2,1)} %constant.30.clone.second_ref) | copy-start | bytes 393220

commit v2 on v1

--- a/solution.py
+++ b/solution.py
@@ -68,19 +68,26 @@
     return lax.dot_general(left, right, (((1,), (1,)), ((), ())), preferred_element_type=jnp.float32)
 
 
-def forward_kernel(x_ref, first_ref, second_ref, ct_ref, st_ref, o_ref, held):
+def forward_kernel(x_ref, first_ref, second_ref, ct_ref, st_ref, o_ref, held, lines):
     rows = x_ref.shape[2]
     members, _, per, _, _ = o_ref.shape
+    fold = x_ref.shape[3] // LOW
+    for p in range(2):
+        for s in range(members):
+            tall = jnp.stack(
+                [
+                    x_ref[s, p, :, a * LOW : (a + 1) * LOW].astype(jnp.float32)
+                    for a in range(fold)
+                ]
+            )
+            lo = p * HIGH + s * fold
+            lines[:, lo : lo + fold, :] = jnp.swapaxes(tall, 0, 1)
 
     def pair(index, carry):
         both = []
         for j in range(2):
             r = index * 2 + j
-            both.append(
-                jnp.concatenate(
-                    [x_ref[:, p, r].reshape(HIGH, LOW) for p in range(2)], axis=0
-                )
-            )
+            both.append(lines[r].astype(jnp.bfloat16))
         y = dot(first_ref[...], jnp.concatenate(both, axis=1))
         for j in range(2):
             yr = y[:HIGH, j * LOW : (j + 1) * LOW]
@@ -104,7 +111,7 @@
             o_ref[d, p] = piece.astype(jnp.bfloat16)
 
 
-def inverse_kernel(x_ref, second_ref, first_ref, ct_ref, st_ref, o_ref, held):
+def inverse_kernel(x_ref, second_ref, first_ref, ct_ref, st_ref, o_ref, held, lines):
     members, _, per, rows, _ = x_ref.shape
     group = max(1, 16 // per)
     for p in range(2):
@@ -131,13 +138,18 @@
                     axis=1,
                 )
             )
-        out = dot_t(first_ref[...], jnp.concatenate(both, axis=0)).astype(jnp.bfloat16)
-        for p in range(2):
-            for j in range(2):
-                o_ref[p, index * 2 + j] = out[p * HIGH : (p + 1) * HIGH, j * LOW : (j + 1) * LOW]
+        out = dot_t(first_ref[...], jnp.concatenate(both, axis=0))
+        for j in range(2):
+            lines[index * 2 + j] = out[:, j * LOW : (j + 1) * LOW]
         return carry
 
     lax.fori_loop(0, rows // 2, pair, 0)
+    for p in range(2):
+        for a in range(0, HIGH, 16):
+            lo = p * HIGH + a
+            wide = jnp.swapaxes(lines[:, lo : lo + 16, :], 0, 1).astype(jnp.bfloat16)
+            for b in range(16):
+                o_ref[p, :, (a + b) * LOW : (a + b + 1) * LOW] = wide[b]
 
 
 def migrate_kernel(
@@ -215,14 +227,14 @@
 
 
 def forward(x, first, second, ct, st):
-    members, _, columns, fold, _ = x.shape
+    members, _, columns, length = x.shape
     per = LOW // members
     rows = min(16, columns)
     return pl.pallas_call(
         forward_kernel,
         grid=(columns // rows,),
         in_specs=[
-            pl.BlockSpec((members, 2, rows, fold, LOW), lambda i: (0, 0, i, 0, 0)),
+            pl.BlockSpec((members, 2, rows, length), lambda i: (0, 0, i, 0)),
             whole_spec(first.shape),
             whole_spec(second.shape),
             whole_spec(ct.shape),
@@ -230,7 +242,10 @@
         ],
         out_specs=pl.BlockSpec((members, 2, per, rows, HIGH), lambda i: (0, 0, 0, i, 0)),
         out_shape=jax.ShapeDtypeStruct((members, 2, per, columns, HIGH), jnp.bfloat16),
-        scratch_shapes=[pltpu.VMEM((rows, 2 * LOW, HIGH), jnp.float32)],
+        scratch_shapes=[
+            pltpu.VMEM((rows, 2 * LOW, HIGH), jnp.float32),
+            pltpu.VMEM((rows, 2 * HIGH, LOW), jnp.float32),
+        ],
         compiler_params=params(),
     )(x, first, second, ct, st)
 
@@ -248,9 +263,12 @@
             whole_spec(ct.shape),
             whole_spec(st.shape),
         ],
-        out_specs=pl.BlockSpec((2, rows, HIGH, LOW), lambda i: (0, i, 0, 0)),
-        out_shape=jax.ShapeDtypeStruct((2, columns, HIGH, LOW), jnp.bfloat16),
-        scratch_shapes=[pltpu.VMEM((rows, 2 * LOW, HIGH), jnp.bfloat16)],
+        out_specs=pl.BlockSpec((2, rows, A), lambda i: (0, i, 0)),
+        out_shape=jax.ShapeDtypeStruct((2, columns, A), jnp.bfloat16),
+        scratch_shapes=[
+            pltpu.VMEM((rows, 2 * LOW, HIGH), jnp.bfloat16),
+            pltpu.VMEM((rows, 2 * HIGH, LOW), jnp.float32),
+        ],
         compiler_params=params(),
     )(x, second, first, ct, st)
 
@@ -294,7 +312,7 @@
     range_rows, lines = echoes.shape[1:]
     columns = range_rows // members
     per = LOW // members
-    grouped = echoes.reshape(2, members, columns, lines // LOW, LOW).transpose(1, 0, 2, 3, 4)
+    grouped = echoes.reshape(2, members, columns, lines).transpose(1, 0, 2, 3)
     spectrum = exchange(forward(exchange(grouped), first, second, ct, st))
     chunks = HT * TILE // columns
     count = lax.axis_size("rg")
@@ -307,7 +325,7 @@
         place, kern_id, band_lo, band_width, low, spectrum, high, coef_table, rate
     )
     image = inverse(exchange(focused), second_back, first_back, ct_back, st_back)
-    return image.reshape(2, columns, A)
+    return image
 
 
 def solution(mesh):

time: 692 us -> 674 us (0.974)
  local copies, waits for them, and re-layouts: 37.4 us -> 14 us
    reshape x2 -> x1, local copies, waits for them, and re-layouts: 21.7 us -> 7.89 us  [body(): grouped = echoes.reshape(2, members, columns, lines).transpose(1, 0, 2, 3)]
    unnamed x29 -> x28, local copies, waits for them, and re-layouts: 11.7 us -> 2.14 us
where the time goes in v2:
time: 674 us; the launch traced here: 673 us
  blocking collectives  527 us (78%)
  Pallas kernels  79.9 us (12%)
  waiting for transfers between devices  45.6 us (7%)
  local copies, waits for them, and re-layouts  14 us (2%)
    all_to_all x3, blocking collectives, exchange(): return lax.all_to_all(block, 'az', split_axis=0, concat_axis=0, tiled=True)  527 us
    ppermute x1, waiting for transfers between devices, body(): high = lax.ppermute(spectrum[:chunks], 'rg', down)  41.8 us
    pallas_call x1, Pallas kernels, forward(): pl.pallas_call(forward_kernel, grid=(columns // rows,), in_specs=[pl.Bloc...  29.3 us
    pallas_call x1, Pallas kernels, inverse(): pl.pallas_call(inverse_kernel, grid=(columns // rows,), in_specs=[pl.Bloc...  27.4 us
    pallas_call x1, Pallas kernels, migrate(): pl.pallas_call(migrate_kernel, grid_spec=pltpu.PrefetchScalarGridSpec(num...  23.3 us
  transfers between devices with their start and end apart: 2, of which 2 were waited for; matrix products, arithmetic and copies ran while one was open for 0% of the time, Pallas kernels for 0%

profile of v2, /device:TPU:6, one launch (start us, length us, event | category | flops | bytes accessed | tf_op | source)
XLA Modules:
  0.0 673.0 jit_solution(1644762602991941190)
XLA Ops:
  0.0 7.9 %copy.18 = bf16[2,8,64,4096]{3,2,0,1:T(8,128)(2,1)} copy(bf16[2,8,64,4096]{3,2,1,0:T(8,128)(2,1)} %bitcast.7) | data formatting | bytes 16777216 | tf_op jit(solution)/shard_map/reshape | solution.py:315
  7.9 189.1 %all_to_all.15.x_ref = bf16[8,2,64,4096]{3,2,1,0:T(8,128)(2,1)} all-to-all(bf16[8,2,64,4096]{3,2,1,0:T(8,128)(2,1)} %bitcast.6), channel_id=1, replica_groups=mesh['az'=8,'rg'=4] {'az'}, dimensions={0} | all-to-all | bytes 16777216 | tf_op jit(solution)/shard_map/all_to_all | solution.py:305
  197.0 0.0 copy-done.2
  197.0 0.0 copy-done.6
  197.0 0.0 copy-done.7
  197.0 0.0 copy-done.8
  197.0 29.3 %shard_map.136 = bf16[8,2,16,64,256]{4,3,2,1,0:T(8,128)(2,1)} custom-call(bf16[8,2,64,4096]{3,2,1,0:T(8,128)(2,1)} %all_to_all.15.x_ref, bf16[512,512]{1,0:T(8,128)(2,1)S(1)} %copy-done.2, bf16[256,256]{1,0:T(8,128)(2,1)S(1)} %copy-done.8, f32[256,128]{1,0:T(8,128)S(1)} %copy-done.7, f32[256,128]{1,0:T(8,128)S(1)} %copy-done.6), custom_call_target="tpu_custom_call" | custom-call | tf_op jit(solution)/shard_map/pallas_call | solution.py:233
  226.3 186.5 %all_to_all.16.mid_ref = bf16[8,2,16,64,256]{4,3,2,1,0:T(8,128)(2,1)S(1)} all-to-all(bf16[8,2,16,64,256]{4,3,2,1,0:T(8,128)(2,1)} %shard_map.136), channel_id=1, replica_groups=mesh['az'=8,'rg'=4] {'az'}, dimensions={0} | all-to-all | bytes 16777216 | tf_op jit(solution)/shard_map/all_to_all | solution.py:305
  412.8 0.0 copy-start.10
  412.8 0.0 copy-start.11
  412.8 3.8 fusion
  416.7 2.1 copy-done.12
  418.7 1.9 collective-permute-start.1
  420.6 4.3 collective-permute-start
  425.0 0.0 copy-done.13
  425.0 0.1 copy.16.rate_ref
  425.2 41.8 %collective-permute-done.1.high_ref = bf16[4,2,16,64,256]{4,3,2,1,0:T(8,128)(2,1)} collective-permute-done((bf16[4,2,16,64,256]{4,3,2,1,0:T(8,128)(2,1)}, bf16[4,2,16,64,256]{4,3,2,1,0:T(8,128)(2,1)}, u32[]{:S(2)}, u32[]{:S(2)}) %collective-permute-start.1) | collective-permute-done | bytes 4194336 | tf_op jit(solution)/shard_map/ppermute | solution.py:322
  467.0 3.8 collective-permute-done.low_ref
  470.8 0.0 copy-done
  470.8 23.3 %shard_map.137 = bf16[8,2,16,64,256]{4,3,2,1,0:T(8,128)(2,1)} custom-call(s32[1]{0:T(128)} %bitcast.place, s32[256]{0:T(256)S(1)} %copy-done.9, s32[256]{0:T(256)S(1)} %copy-done.10, s32[256]{0:T(256)S(1)} %copy-done.11, bf16[4,2,16,64,256]{4,3,2,1,0:T(8,128)(2,1)} %collective-permute-done.low_ref, bf16[8,2,16,64,256]{4,3,2,1,0:T(8,128)(2,1)} %copy-done.12, ...), custom_call_target="tpu_custom_call" | custom-call | tf_op jit(solution)/shard_map/pallas_call | solution.py:284
  494.1 0.0 copy-start.5
  494.1 151.5 %all_to_all.17.x_ref = bf16[8,2,16,64,256]{4,3,2,1,0:T(8,128)(2,1)} all-to-all(bf16[8,2,16,64,256]{4,3,2,1,0:T(8,128)(2,1)} %shard_map.137), channel_id=1, replica_groups=mesh['az'=8,'rg'=4] {'az'}, dimensions={0} | all-to-all | bytes 16777216 | tf_op jit(solution)/shard_map/all_to_all | solution.py:305
  645.6 0.0 copy-done.4
  645.7 27.4 %shard_map.138 = bf16[2,64,32768]{2,1,0:T(8,128)(2,1)} custom-call(bf16[8,2,16,64,256]{4,3,2,1,0:T(8,128)(2,1)} %all_to_all.17.x_ref, bf16[256,256]{1,0:T(8,128)(2,1)S(1)} %copy-done.5, bf16[512,512]{1,0:T(8,128)(2,1)S(1)} %copy-done.1, f32[128,256]{1,0:T(8,128)S(1)} %copy-done.4, f32[128,256]{1,0:T(8,128)S(1)} %copy-done.3), custom_call_target="tpu_custom_call" | custom-call | tf_op jit(solution)/shard_map/pallas_call | solution.py:256
  (17 shorter events, 0.0 us)
Async XLA Ops:
  7.9 189.1 %copy-start.2 = (bf16[512,512]{1,0:T(8,128)(2,1)S(1)}, bf16[512,512]{1,0:T(8,128)(2,1)}, u32[]{:S(2)}) copy-start(bf16[512,512]{1,0:T(8,128)(2,1)} %constant.26.clone.first_ref) | copy-start | bytes 1572868
  7.9 189.1 %copy-start.6 = (f32[256,128]{1,0:T(8,128)S(1)}, f32[256,128]{1,0:T(8,128)}, u32[]{:S(2)}) copy-start(f32[256,128]{1,0:T(8,128)} %constant.29.clone.st_ref) | copy-start | bytes 393220
  7.9 189.1 %copy-start.7 = (f32[256,128]{1,0:T(8,128)S(1)}, f32[256,128]{1,0:T(8,128)}, u32[]{:S(2)}) copy-start(f32[256,128]{1,0:T(8,128)} %constant.28.clone.ct_ref) | copy-start | bytes 393220
  7.9 189.1 %copy-start.8 = (bf16[256,256]{1,0:T(8,128)(2,1)S(1)}, bf16[256,256]{1,0:T(8,128)(2,1)}, u32[]{:S(2)}) copy-start(bf16[256,256]{1,0:T(8,128)(2,1)} %constant.27.clone.second_ref) | copy-start | bytes 393220
  412.8 5.9 copy-start.12
  412.8 12.2 %copy-start.13 = (f32[512]{0:T(512)S(1)}, f32[512]{0:T(512)}, u32[]{:S(2)}) copy-start(f32[512]{0:T(512)} %param.19) | copy-start | bytes 6148
  412.8 58.0 %copy-start = (bf16[8,5,128,128]{3,2,1,0:T(8,128)(2,1)S(1)}, bf16[8,5,128,128]{3,2,1,0:T(8,128)(2,1)}, u32[]{:S(2)}) copy-start(bf16[8,5,128,128]{3,2,1,0:T(8,128)(2,1)} %coef_ref.1) | copy-start | bytes 3932164
  412.8 58.0 %copy-start.9 = (s32[256]{0:T(256)S(1)}, s32[256]{0:T(256)}, u32[]{:S(2)}) copy-start(s32[256]{0:T(256)} %kern_id.1) | copy-start | bytes 3076
  412.8 58.0 %copy-start.10 = (s32[256]{0:T(256)S(1)}, s32[256]{0:T(256)}, u32[]{:S(2)}) copy-start(s32[256]{0:T(256)} %band_lo.1) | copy-start | bytes 3076
  412.8 58.0 %copy-start.11 = (s32[256]{0:T(256)S(1)}, s32[256]{0:T(256)}, u32[]{:S(2)}) copy-start(s32[256]{0:T(256)} %band_width.1) | copy-start | bytes 3076
  418.7 48.2 %collective-permute-start.1 = (bf16[4,2,16,64,256]{4,3,2,1,0:T(8,128)(2,1)}, bf16[4,2,16,64,256]{4,3,2,1,0:T(8,128)(2,1)}, u32[]{:S(2)}, u32[]{:S(2)}) collective-permute-start(bf16[4,2,16,64,256]{4,3,2,1,0:T(8,128)(2,1)} %get-tuple-element.5), channel_id=1, source_target_pairs={{1,0},{2,1},{3,2},{5,4},{6,5},{7,6},{9,8},{10,9},{11,10},{13,12},{... | collective-permute-start | bytes 12582920 | tf_op jit(solution)/shard_map/ppermute | solution.py:322
  420.6 50.1 %collective-permute-start = (bf16[4,2,16,64,256]{4,3,2,1,0:T(8,128)(2,1)}, bf16[4,2,16,64,256]{4,3,2,1,0:T(8,128)(2,1)}, u32[]{:S(2)}, u32[]{:S(2)}) collective-permute-start(bf16[4,2,16,64,256]{4,3,2,1,0:T(8,128)(2,1)} %get-tuple-element.6), channel_id=1, source_target_pairs={{0,1},{1,2},{2,3},{4,5},{5,6},{6,7},{8,9},{9,10},{10,11},{12,13},{... | collective-permute-start | bytes 12582920 | tf_op jit(solution)/shard_map/ppermute | solution.py:321
  494.1 151.6 %copy-start.1 = (bf16[512,512]{1,0:T(8,128)(2,1)S(1)}, bf16[512,512]{1,0:T(8,128)(2,1)}, u32[]{:S(2)}) copy-start(bf16[512,512]{1,0:T(8,128)(2,1)} %constant.31.clone.first_ref) | copy-start | bytes 1572868
  494.1 151.6 %copy-start.3 = (f32[128,256]{1,0:T(8,128)S(1)}, f32[128,256]{1,0:T(8,128)}, u32[]{:S(2)}) copy-start(f32[128,256]{1,0:T(8,128)} %constant.33.clone.st_ref) | copy-start | bytes 393220
  494.1 151.6 %copy-start.4 = (f32[128,256]{1,0:T(8,128)S(1)}, f32[128,256]{1,0:T(8,128)}, u32[]{:S(2)}) copy-start(f32[128,256]{1,0:T(8,128)} %constant.32.clone.ct_ref) | copy-start | bytes 393220
  494.1 151.6 %copy-start.5 = (bf16[256,256]{1,0:T(8,128)(2,1)S(1)}, bf16[256,256]{1,0:T(8,128)(2,1)}, u32[]{:S(2)}) copy-start(bf16[256,256]{1,0:T(8,128)(2,1)} %constant.30.clone.second_ref) | copy-start | bytes 393220

commit v3 on v2

--- a/solution.py
+++ b/solution.py
@@ -68,15 +68,16 @@
     return lax.dot_general(left, right, (((1,), (1,)), ((), ())), preferred_element_type=jnp.float32)
 
 
-def forward_kernel(x_ref, first_ref, second_ref, ct_ref, st_ref, o_ref, held, lines):
-    rows = x_ref.shape[2]
+def forward_kernel(real_ref, imaginary_ref, first_ref, second_ref, ct_ref, st_ref, o_ref, held, lines):
+    planes = (real_ref, imaginary_ref)
+    rows = real_ref.shape[1]
     members, _, per, _, _ = o_ref.shape
-    fold = x_ref.shape[3] // LOW
+    fold = real_ref.shape[2] // LOW
     for p in range(2):
         for s in range(members):
             tall = jnp.stack(
                 [
-                    x_ref[s, p, :, a * LOW : (a + 1) * LOW].astype(jnp.float32)
+                    planes[p][s, :, a * LOW : (a + 1) * LOW].astype(jnp.float32)
                     for a in range(fold)
                 ]
             )
@@ -226,15 +227,16 @@
     return pltpu.CompilerParams(vmem_limit_bytes=VMEM)
 
 
-def forward(x, first, second, ct, st):
-    members, _, columns, length = x.shape
+def forward(real, imaginary, first, second, ct, st):
+    members, columns, length = real.shape
     per = LOW // members
     rows = min(16, columns)
     return pl.pallas_call(
         forward_kernel,
         grid=(columns // rows,),
         in_specs=[
-            pl.BlockSpec((members, 2, rows, length), lambda i: (0, 0, i, 0)),
+            pl.BlockSpec((members, rows, length), lambda i: (0, i, 0)),
+            pl.BlockSpec((members, rows, length), lambda i: (0, i, 0)),
             whole_spec(first.shape),
             whole_spec(second.shape),
             whole_spec(ct.shape),
@@ -247,7 +249,7 @@
             pltpu.VMEM((rows, 2 * HIGH, LOW), jnp.float32),
         ],
         compiler_params=params(),
-    )(x, first, second, ct, st)
+    )(real, imaginary, first, second, ct, st)
 
 
 def inverse(x, second, first, ct, st):
@@ -312,8 +314,8 @@
     range_rows, lines = echoes.shape[1:]
     columns = range_rows // members
     per = LOW // members
-    grouped = echoes.reshape(2, members, columns, lines).transpose(1, 0, 2, 3)
-    spectrum = exchange(forward(exchange(grouped), first, second, ct, st))
+    grouped = echoes.reshape(2, members, columns, lines)
+    spectrum = exchange(forward(exchange(grouped[0]), exchange(grouped[1]), first, second, ct, st))
     chunks = HT * TILE // columns
     count = lax.axis_size("rg")
     up = [(i, i + 1) for i in range(count - 1)]

time: 674 us -> 676 us (level)
    reshape x1 -> x0, local copies, waits for them, and re-layouts: 7.89 us -> none  [body(): grouped = echoes.reshape(2, members, columns, lines).transpose(1, 0, 2, 3)]
    all_to_all x3 -> x4, blocking collectives: 527 us -> 533 us  [exchange(): return lax.all_to_all(block, 'az', split_axis=0, concat_axis=0, tiled=True)]
where the time goes in v3:
time: 676 us; the launch traced here: 675 us
  blocking collectives  533 us (79%)
  Pallas kernels  79.8 us (12%)
  waiting for transfers between devices  45.6 us (7%)
  local copies, waits for them, and re-layouts  10 us (1%)
    all_to_all x4, blocking collectives, exchange(): return lax.all_to_all(block, 'az', split_axis=0, concat_axis=0, tiled=True)  533 us
    ppermute x1, waiting for transfers between devices, body(): high = lax.ppermute(spectrum[:chunks], 'rg', down)  41.8 us
    pallas_call x1, Pallas kernels, forward(): pl.pallas_call(forward_kernel, grid=(columns // rows,), in_specs=[pl.Bloc...  29.2 us
    pallas_call x1, Pallas kernels, inverse(): pl.pallas_call(inverse_kernel, grid=(columns // rows,), in_specs=[pl.Bloc...  27.4 us
    pallas_call x1, Pallas kernels, migrate(): pl.pallas_call(migrate_kernel, grid_spec=pltpu.PrefetchScalarGridSpec(num...  23.3 us
  transfers between devices with their start and end apart: 2, of which 2 were waited for; matrix products, arithmetic and copies ran while one was open for 0% of the time, Pallas kernels for 0%

profile of v3, /device:TPU:6, one launch (start us, length us, event | category | flops | bytes accessed | tf_op | source)
XLA Modules:
  0.0 674.9 jit_solution(15514359185143364402)
XLA Ops:
  0.0 4.0 fusion.1
  4.0 98.8 %all_to_all.20.real_ref = bf16[8,64,4096]{2,1,0:T(8,128)(2,1)S(1)} all-to-all(bf16[8,64,4096]{2,1,0:T(8,128)(2,1)S(1)} %bitcast.5), channel_id=1, replica_groups=mesh['az'=8,'rg'=4] {'az'}, dimensions={0} | all-to-all | bytes 8388608 | tf_op jit(solution)/shard_map/all_to_all | solution.py:307
  102.7 96.5 %all_to_all.21.imaginary_ref = bf16[8,64,4096]{2,1,0:T(8,128)(2,1)} all-to-all(bf16[8,64,4096]{2,1,0:T(8,128)(2,1)S(1)} %bitcast.4), channel_id=1, replica_groups=mesh['az'=8,'rg'=4] {'az'}, dimensions={0} | all-to-all | bytes 8388608 | tf_op jit(solution)/shard_map/all_to_all | solution.py:307
  199.2 0.0 copy-done.2
  199.2 0.0 copy-done.6
  199.2 0.0 copy-done.7
  199.2 0.0 copy-done.8
  199.2 29.2 %shard_map.136 = bf16[8,2,16,64,256]{4,3,2,1,0:T(8,128)(2,1)} custom-call(bf16[8,64,4096]{2,1,0:T(8,128)(2,1)S(1)} %all_to_all.20.real_ref, bf16[8,64,4096]{2,1,0:T(8,128)(2,1)} %all_to_all.21.imaginary_ref, bf16[512,512]{1,0:T(8,128)(2,1)S(1)} %copy-done.2, bf16[256,256]{1,0:T(8,128)(2,1)S(1)} %copy-done.8, f32[256,128]{1,0:T(8,128)S(1)} %copy-done.7, ...), custom_call_target="tpu_custom_call" | custom-call | tf_op jit(solution)/shard_map/pallas_call | solution.py:234
  228.4 186.3 %all_to_all.22.mid_ref = bf16[8,2,16,64,256]{4,3,2,1,0:T(8,128)(2,1)S(1)} all-to-all(bf16[8,2,16,64,256]{4,3,2,1,0:T(8,128)(2,1)} %shard_map.136), channel_id=1, replica_groups=mesh['az'=8,'rg'=4] {'az'}, dimensions={0} | all-to-all | bytes 16777216 | tf_op jit(solution)/shard_map/all_to_all | solution.py:307
  414.7 0.0 copy-start.10
  414.7 0.0 copy-start.11
  414.7 3.8 fusion
  418.5 2.1 copy-done.12
  420.6 1.9 collective-permute-start.1
  422.5 4.3 collective-permute-start
  426.8 0.1 copy.15.rate_ref
  427.0 41.8 %collective-permute-done.1.high_ref = bf16[4,2,16,64,256]{4,3,2,1,0:T(8,128)(2,1)} collective-permute-done((bf16[4,2,16,64,256]{4,3,2,1,0:T(8,128)(2,1)}, bf16[4,2,16,64,256]{4,3,2,1,0:T(8,128)(2,1)}, u32[]{:S(2)}, u32[]{:S(2)}) %collective-permute-start.1) | collective-permute-done | bytes 4194336 | tf_op jit(solution)/shard_map/ppermute | solution.py:324
  468.8 3.8 collective-permute-done.low_ref
  472.6 0.0 copy-done
  472.6 23.3 %shard_map.137 = bf16[8,2,16,64,256]{4,3,2,1,0:T(8,128)(2,1)} custom-call(s32[1]{0:T(128)} %bitcast.place, s32[256]{0:T(256)S(1)} %copy-done.9, s32[256]{0:T(256)S(1)} %copy-done.10, s32[256]{0:T(256)S(1)} %copy-done.11, bf16[4,2,16,64,256]{4,3,2,1,0:T(8,128)(2,1)} %collective-permute-done.low_ref, bf16[8,2,16,64,256]{4,3,2,1,0:T(8,128)(2,1)} %copy-done.12, ...), custom_call_target="tpu_custom_call" | custom-call | tf_op jit(solution)/shard_map/pallas_call | solution.py:286
  495.9 0.0 copy-start.5
  495.9 151.6 %all_to_all.23.x_ref = bf16[8,2,16,64,256]{4,3,2,1,0:T(8,128)(2,1)} all-to-all(bf16[8,2,16,64,256]{4,3,2,1,0:T(8,128)(2,1)} %shard_map.137), channel_id=1, replica_groups=mesh['az'=8,'rg'=4] {'az'}, dimensions={0} | all-to-all | bytes 16777216 | tf_op jit(solution)/shard_map/all_to_all | solution.py:307
  647.5 0.0 copy-done.4
  647.6 27.4 %shard_map.138 = bf16[2,64,32768]{2,1,0:T(8,128)(2,1)} custom-call(bf16[8,2,16,64,256]{4,3,2,1,0:T(8,128)(2,1)} %all_to_all.23.x_ref, bf16[256,256]{1,0:T(8,128)(2,1)S(1)} %copy-done.5, bf16[512,512]{1,0:T(8,128)(2,1)S(1)} %copy-done.1, f32[128,256]{1,0:T(8,128)S(1)} %copy-done.4, f32[128,256]{1,0:T(8,128)S(1)} %copy-done.3), custom_call_target="tpu_custom_call" | custom-call | tf_op jit(solution)/shard_map/pallas_call | solution.py:258
  (18 shorter events, 0.0 us)
Async XLA Ops:
  102.7 96.5 %copy-start.2 = (bf16[512,512]{1,0:T(8,128)(2,1)S(1)}, bf16[512,512]{1,0:T(8,128)(2,1)}, u32[]{:S(2)}) copy-start(bf16[512,512]{1,0:T(8,128)(2,1)} %constant.26.clone.first_ref) | copy-start | bytes 1572868
  102.7 96.5 %copy-start.6 = (f32[256,128]{1,0:T(8,128)S(1)}, f32[256,128]{1,0:T(8,128)}, u32[]{:S(2)}) copy-start(f32[256,128]{1,0:T(8,128)} %constant.29.clone.st_ref) | copy-start | bytes 393220
  102.7 96.5 %copy-start.7 = (f32[256,128]{1,0:T(8,128)S(1)}, f32[256,128]{1,0:T(8,128)}, u32[]{:S(2)}) copy-start(f32[256,128]{1,0:T(8,128)} %constant.28.clone.ct_ref) | copy-start | bytes 393220
  102.7 96.5 %copy-start.8 = (bf16[256,256]{1,0:T(8,128)(2,1)S(1)}, bf16[256,256]{1,0:T(8,128)(2,1)}, u32[]{:S(2)}) copy-start(bf16[256,256]{1,0:T(8,128)(2,1)} %constant.27.clone.second_ref) | copy-start | bytes 393220
  414.6 5.9 copy-start.12
  414.6 12.2 %copy-start.13 = (f32[512]{0:T(512)S(1)}, f32[512]{0:T(512)}, u32[]{:S(2)}) copy-start(f32[512]{0:T(512)} %param.19) | copy-start | bytes 6148
  414.6 58.0 %copy-start = (bf16[8,5,128,128]{3,2,1,0:T(8,128)(2,1)S(1)}, bf16[8,5,128,128]{3,2,1,0:T(8,128)(2,1)}, u32[]{:S(2)}) copy-start(bf16[8,5,128,128]{3,2,1,0:T(8,128)(2,1)} %coef_ref.1) | copy-start | bytes 3932164
  414.7 58.0 %copy-start.9 = (s32[256]{0:T(256)S(1)}, s32[256]{0:T(256)}, u32[]{:S(2)}) copy-start(s32[256]{0:T(256)} %kern_id.1) | copy-start | bytes 3076
  414.7 58.0 %copy-start.10 = (s32[256]{0:T(256)S(1)}, s32[256]{0:T(256)}, u32[]{:S(2)}) copy-start(s32[256]{0:T(256)} %band_lo.1) | copy-start | bytes 3076
  414.7 58.0 %copy-start.11 = (s32[256]{0:T(256)S(1)}, s32[256]{0:T(256)}, u32[]{:S(2)}) copy-start(s32[256]{0:T(256)} %band_width.1) | copy-start | bytes 3076
  420.6 48.2 %collective-permute-start.1 = (bf16[4,2,16,64,256]{4,3,2,1,0:T(8,128)(2,1)}, bf16[4,2,16,64,256]{4,3,2,1,0:T(8,128)(2,1)}, u32[]{:S(2)}, u32[]{:S(2)}) collective-permute-start(bf16[4,2,16,64,256]{4,3,2,1,0:T(8,128)(2,1)} %get-tuple-element.5), channel_id=1, source_target_pairs={{1,0},{2,1},{3,2},{5,4},{6,5},{7,6},{9,8},{10,9},{11,10},{13,12},{... | collective-permute-start | bytes 12582920 | tf_op jit(solution)/shard_map/ppermute | solution.py:324
  422.5 50.1 %collective-permute-start = (bf16[4,2,16,64,256]{4,3,2,1,0:T(8,128)(2,1)}, bf16[4,2,16,64,256]{4,3,2,1,0:T(8,128)(2,1)}, u32[]{:S(2)}, u32[]{:S(2)}) collective-permute-start(bf16[4,2,16,64,256]{4,3,2,1,0:T(8,128)(2,1)} %get-tuple-element.6), channel_id=1, source_target_pairs={{0,1},{1,2},{2,3},{4,5},{5,6},{6,7},{8,9},{9,10},{10,11},{12,13},{... | collective-permute-start | bytes 12582920 | tf_op jit(solution)/shard_map/ppermute | solution.py:323
  495.9 151.6 %copy-start.1 = (bf16[512,512]{1,0:T(8,128)(2,1)S(1)}, bf16[512,512]{1,0:T(8,128)(2,1)}, u32[]{:S(2)}) copy-start(bf16[512,512]{1,0:T(8,128)(2,1)} %constant.31.clone.first_ref) | copy-start | bytes 1572868
  495.9 151.6 %copy-start.3 = (f32[128,256]{1,0:T(8,128)S(1)}, f32[128,256]{1,0:T(8,128)}, u32[]{:S(2)}) copy-start(f32[128,256]{1,0:T(8,128)} %constant.33.clone.st_ref) | copy-start | bytes 393220
  495.9 151.6 %copy-start.4 = (f32[128,256]{1,0:T(8,128)S(1)}, f32[128,256]{1,0:T(8,128)}, u32[]{:S(2)}) copy-start(f32[128,256]{1,0:T(8,128)} %constant.32.clone.ct_ref) | copy-start | bytes 393220
  495.9 151.6 %copy-start.5 = (bf16[256,256]{1,0:T(8,128)(2,1)S(1)}, bf16[256,256]{1,0:T(8,128)(2,1)}, u32[]{:S(2)}) copy-start(bf16[256,256]{1,0:T(8,128)(2,1)} %constant.30.clone.second_ref) | copy-start | bytes 393220
